TPU v7x, 128 devices: a whole 4x4x4 slice. The times are simulated.
128 devices in a mesh: row: 16 (over y, x), col: 8 (over z, core).
Axes of the slice: x: 4, y: 4, z: 4, core: 2. Of those that a mesh axis runs over, the one named last changes fastest.
Arguments:
- inputs: bfloat16 [512, 16384], P('col', 'row'), may hold values from -6 to 6
- gate_weight: bfloat16 [16384, 26624], P('row', 'col'), may hold values from -0.0625 to 0.0625
- up_weight: bfloat16 [16384, 26624], P('row', 'col'), may hold values from -0.0625 to 0.0625
- gate_pattern: int32 [128, 208], P('row', 'col'), may hold values 0 or 1
- up_pattern: int32 [128, 208], P('row', 'col'), may hold values 0 or 1
- cotangent: bfloat16 [512, 26624], P('row', 'col'), may hold values from -6 to 6
Outputs:
- hidden: bfloat16 [512, 26624], P('row', 'col')
- input_grad: bfloat16 [512, 16384], P('col', 'row')
All inputs are finite; a program needn't handle non-finite values. No bound on the sum of `gate_pattern` or of `up_pattern` on one device may be relied on, other than what follows from the above.
Results may differ from a plain program's by a relative error of at most 0.039.
Values may be sent and summed in bfloat16 or wider, within the bound.
A program may use at most 128 MiB of HBM per device.

v0:
```python
import jax
import jax.numpy as jnp
from jax import lax
from jax.sharding import PartitionSpec as P

BLOCK = 128


def expand(weight, pattern):
    height, breadth = weight.shape
    flags = pattern.astype(weight.dtype)
    tiles = (
        weight.reshape(height // BLOCK, BLOCK, breadth // BLOCK, BLOCK) * flags[:, None, :, None]
    )
    return tiles.reshape(height, breadth)


def derivatives(summed, cotangent, local_hidden):
    gate_sum = summed[:, :local_hidden]
    up_sum = summed[:, local_hidden:]
    sigmoid_gate = jax.nn.sigmoid(gate_sum)
    activated = gate_sum * sigmoid_gate
    hidden = (activated * up_sum).astype(jnp.bfloat16)
    cotangent_f = cotangent.astype(jnp.float32)
    gate_grad = (
        cotangent_f * up_sum * sigmoid_gate * (1.0 + gate_sum * (1.0 - sigmoid_gate))
    ).astype(jnp.bfloat16)
    up_grad = (cotangent_f * activated).astype(jnp.bfloat16)
    return (hidden, jnp.concatenate([gate_grad, up_grad], axis=1))


def shards(inputs, gate_weight, up_weight, gate_pattern, up_pattern, cotangent):
    local_hidden = gate_weight.shape[1]
    stacked_weights = jnp.concatenate(
        [expand(gate_weight, gate_pattern), expand(up_weight, up_pattern)], axis=1
    )
    partial_sums = jnp.dot(
        lax.all_gather(inputs, "col", axis=0, tiled=True),
        stacked_weights,
        preferred_element_type=jnp.float32,
    )
    summed = lax.psum_scatter(
        partial_sums.astype(jnp.bfloat16), "row", scatter_dimension=0, tiled=True
    ).astype(jnp.float32)
    hidden, gradients = derivatives(summed, cotangent, local_hidden)
    gradient_term = lax.dot_general(
        lax.all_gather(gradients, "row", axis=0, tiled=True),
        stacked_weights,
        (((1,), (1,)), ((), ())),
        preferred_element_type=jnp.float32,
    )
    input_grad = lax.psum_scatter(
        gradient_term.astype(jnp.bfloat16), "col", scatter_dimension=0, tiled=True
    )
    return (hidden, input_grad)


def solution(mesh):
    placed = (
        P("col", "row"),
        P("row", "col"),
        P("row", "col"),
        P("row", "col"),
        P("row", "col"),
        P("row", "col"),
    )
    return jax.shard_map(
        shards,
        mesh=mesh,
        in_specs=placed,
        out_specs=(P("row", "col"), P("col", "row")),
        check_vma=False,
    )
```

profile of v0, /device:TPU:0, one launch (start us, length us, event | category | flops | bytes accessed | tf_op | source)
XLA Modules:
  0.0 266.9 jit_solution(16619707764089216029)
XLA Ops:
  7.2 0.0 all-gather.3.cloned.1.call-start
  7.2 0.7 all-gather.3.cloned.1.call-update
  7.9 0.0 reduce-scatter.7.cloned.1.call-start
  7.9 0.7 convert_element_type.30
  8.6 0.1 copy.24
  8.7 0.7 convert_element_type.31
  9.4 0.1 copy.26
  9.5 9.9 %copy.25 = bf16[1024,3328]{0,1:T(8,128)(2,1)} copy(bf16[1024,3328]{1,0:T(8,128)(2,1)} %param.7) | data formatting | bytes 13631488 | tf_op args[1]
  19.4 0.0 slice-start
  19.4 10.1 %copy.27 = bf16[1024,3328]{0,1:T(8,128)(2,1)} copy(bf16[1024,3328]{1,0:T(8,128)(2,1)} %param.8) | data formatting | bytes 13631488 | tf_op args[2]
  29.5 0.0 slice-start.1
  29.6 0.0 copy-start
  29.6 0.9 mul.43
  30.5 0.9 mul.46
  31.5 0.0 slice-done
  31.5 0.4 slice-done.1
  31.8 2.0 copy-done
  33.9 5.7 %bitcast_multiply_fusion = (bf16[1024,3328]{0,1:T(8,128)(2,1)}, bf16[1024,3328]{0,1:T(8,128)(2,1)}) fusion(bf16[1024,3328]{0,1:T(8,128)(2,1)S(1)} %copy-done, bf16[416,8,8,128]{3,2,1,0:T(8,128)(2,1)S(1)} %bitcast.20, bf16[1024,3328]{0,1:T(8,128)(2,1)S(1)} %bitcast.18, bf16[416,8,8,128]{3,2,1,0:T(8,128)(2,1)S(1)} %bitcast.19), kind=kLoop, calls=%fused_computation.4 | loop fusion | flops 6815744 | bytes 40894464 | tf_op jit(solution)/shard_map/mul | solution.py:13
  39.6 0.0 all-gather.3.cloned.1.call-done
  39.6 15.2 %fusion = bf16[512,6656]{0,1:T(8,128)(2,1)} fusion(bf16[512,1024]{1,0:T(8,128)(2,1)} %all-gather.3.cloned.1.call-done, bf16[1024,3328]{0,1:T(8,128)(2,1)} %get-tuple-element.11, bf16[1024,3328]{0,1:T(8,128)(2,1)} %get-tuple-element.12), kind=kOutput, calls=%fused_computation.2 | convolution fusion | flops 7009992704 | bytes 21495808 | tf_op jit(solution)/shard_map/dot_general | solution.py:37
  54.7 9.9 %copy.29 = bf16[512,6656]{1,0:T(8,128)(2,1)} copy(bf16[512,6656]{0,1:T(8,128)(2,1)} %fusion) | data formatting | bytes 13631488
  64.6 0.0 copy-start.1
  64.6 0.0 reduce-scatter.7.cloned.1.call-update
  64.7 0.0 all-gather.5.cloned.1.call-start
  64.7 84.7 %reduce-scatter.7.cloned.1.call-done = bf16[32,6656]{1,0:T(8,128)(2,1)} async-done(((bf16[512,6656]{1,0:T(8,128)(2,1)}), bf16[32,6656]{1,0:T(8,128)(2,1)}) %reduce-scatter.7.cloned.1.call-update) | async-done | bytes 426000 | tf_op jit(solution)/shard_map/reduce_scatter | solution.py:42
  149.4 1.1 convert_element_type.34
  150.4 0.0 copy-done.1
  150.5 0.9 fusion.5
  151.4 0.8 pad_maximum_fusion.5
  152.2 0.0 all-gather.5.cloned.1.call-update
  152.2 0.0 reduce-scatter.5.cloned.1.call-start
  152.2 63.0 %all-gather.5.cloned.1.call-done = bf16[512,6656]{1,0:T(8,128)(2,1)} async-done(((bf16[32,6656]{1,0:T(8,128)(2,1)}), bf16[512,6656]{1,0:T(8,128)(2,1)}) %all-gather.5.cloned.1.call-update) | async-done | bytes 6815760 | tf_op jit(solution)/shard_map/all_gather | solution.py:47
  215.2 13.1 %fusion.2 = bf16[512,1024]{1,0:T(8,128)(2,1)} fusion(bf16[512,6656]{1,0:T(8,128)(2,1)} %all-gather.5.cloned.1.call-done, bf16[1024,3328]{0,1:T(8,128)(2,1)} %get-tuple-element.11, bf16[1024,3328]{0,1:T(8,128)(2,1)} %get-tuple-element.12), kind=kOutput, calls=%fused_computation.6 | convolution fusion | flops 7007109120 | bytes 21495808 | tf_op jit(solution)/shard_map/dot_general | solution.py:46
  228.3 0.0 reduce-scatter.5.cloned.1.call-update
  228.4 32.0 %reduce-scatter.5.cloned.1.call-done = bf16[64,1024]{1,0:T(8,128)(2,1)} async-done(((bf16[512,1024]{1,0:T(8,128)(2,1)}), bf16[64,1024]{1,0:T(8,128)(2,1)}) %reduce-scatter.5.cloned.1.call-update) | async-done | bytes 131088 | tf_op jit(solution)/shard_map/reduce_scatter | solution.py:52
  (1 shorter events, 0.0 us)
Async XLA Ops:
  7.2 32.4 %all-gather.3.cloned.1.call-start = ((), (), s32[]{:S(2)}) async-start(), calls=%async_computation.2 | async-start | bytes 1179648 | tf_op jit(solution)/shard_map/all_gather | solution.py:38
  7.9 141.5 %reduce-scatter.7.cloned.1.call-start = ((), (), s32[]{:S(2)}) async-start(), calls=%async_computation.5 | async-start | bytes 7241728 | tf_op jit(solution)/shard_map/reduce_scatter | solution.py:42
  19.4 12.0 %slice-start = ((s8[6815744]{0:T(1024)(128)(4,1)}), s8[2621440]{0:T(1024)(128)(4,1)S(1)}, s32[]{:S(2)}) async-start(s8[6815744]{0:T(1024)(128)(4,1)} %bitcast.17), calls=%async_computation.6 | async-start | bytes 5242880
  29.5 2.3 slice-start.1
  29.6 4.3 %copy-start = (bf16[1024,3328]{0,1:T(8,128)(2,1)S(1)}, bf16[1024,3328]{0,1:T(8,128)(2,1)}, u32[]{:S(2)}) copy-start(bf16[1024,3328]{0,1:T(8,128)(2,1)} %copy.27) | copy-start | bytes 20447236
  64.6 85.8 %copy-start.1 = (bf16[32,3328]{1,0:T(8,128)(2,1)S(1)}, bf16[32,3328]{1,0:T(8,128)(2,1)}, u32[]{:S(2)}) copy-start(bf16[32,3328]{1,0:T(8,128)(2,1)} %param.11) | copy-start | bytes 638980
  64.7 150.5 %all-gather.5.cloned.1.call-start = ((), (), s32[]{:S(2)}) async-start(), calls=%async_computation.3 | async-start | bytes 7241728 | tf_op jit(solution)/shard_map/all_gather | solution.py:47
  152.2 108.2 %reduce-scatter.5.cloned.1.call-start = ((), (), s32[]{:S(2)}) async-start(), calls=%async_computation.4 | async-start | bytes 1179648 | tf_op jit(solution)/shard_map/reduce_scatter | solution.py:52
Sparse Core Ops, SparseCore 0:
  9.7 26.0 all-gather.2
  64.8 84.5 reduce-scatter.6
  152.3 62.8 all-gather.4
  228.5 31.8 reduce-scatter.4
where the time goes:
time: 268 us; the launch traced here: 267 us
  waiting for transfers between devices  180 us (67%)
  local copies, waits for them, and re-layouts  34.4 us (13%)
  matrix products  28.3 us (11%)
  between operations  13.8 us (5%)
  other arithmetic  9.88 us (4%)
    reduce_scatter x1, waiting for transfers between devices, shards(): lax.psum_scatter(partial_sums.astype(jnp.bfloat16), 'row', scatter_dimens...  84.7 us
    all_gather x1, waiting for transfers between devices, shards(): lax.all_gather(gradients, 'row', axis=0, tiled=True)  63 us
    unnamed x11, local copies, waits for them, and re-layouts  32.3 us
    reduce_scatter x1, waiting for transfers between devices, shards(): lax.psum_scatter(gradient_term.astype(jnp.bfloat16), 'col', scatter_dimen...  32 us
    dot_general x1, matrix products, shards(): jnp.dot(lax.all_gather(inputs, 'col', axis=0, tiled=True), stacked_weight...  15.2 us
    dot_general x1, matrix products, shards(): lax.dot_general(lax.all_gather(gradients, 'row', axis=0, tiled=True), sta...  13.1 us
    mul x1, other arithmetic, expand(): weight.reshape(height // BLOCK, BLOCK, breadth // BLOCK, BLOCK)  5.73 us
  transfers between devices with their start and end apart: 4, of which 3 were waited for; matrix products, arithmetic and copies ran while one was open for 11% of the time, Pallas kernels for 0%

commit v1 on v0

v1 whole, which is shorter than its diff:
```python
import functools

import jax
import jax.numpy as jnp
from jax import lax
from jax.experimental import pallas as pl
from jax.experimental.pallas import tpu as pltpu
from jax.sharding import PartitionSpec as P

BLOCK = 128
SIDE = 4
CHUNK = 256
PIECES = 4
LAGS = (0, 1, 2, 3, 4, 5, 6, 7, 8)
F32 = jnp.float32
BF16 = jnp.bfloat16


def kernel(
    chunks, inputs, gate_w, up_w, gate_pat, up_pat, cot, hidden_out, grad_out,
    toks, weights, part, half1, full1, sum1, half2, full2, grads, acc, zsend, zsib, zhalf, zfull,
    cot_v, hid_v, out_v, send, recv, zs, zr, ws, cs, hs, os,
):
    ch = CHUNK
    hc = ch // 2
    row, col = lax.axis_index("row"), lax.axis_index("col")
    y, x = row // SIDE, row % SIDE
    z, core = col // 2, col % 2
    ym, yp, y2 = (y + 3) % SIDE, (y + 1) % SIDE, (y + 2) % SIDE
    xm, xp, x2 = (x + 3) % SIDE, (x + 1) % SIDE, (x + 2) % SIDE
    zm, zp, z2 = (z + 3) % SIDE, (z + 1) % SIDE, (z + 2) % SIDE
    other = 1 - core

    def at(yy, xx):
        return (yy * SIDE + xx, col)

    def atz(zz, cc):
        return (row, zz * 2 + cc)

    left_x, right_x, left_y, right_y = at(y, xm), at(y, xp), at(ym, x), at(yp, x)
    left_z, right_z, sibling = atz(zm, core), atz(zp, core), atz(z, other)

    def remote(src, dst, s, r, dev):
        return pltpu.make_async_remote_copy(
            src_ref=src, dst_ref=dst, send_sem=s, recv_sem=r,
            device_id=dev, device_id_type=pl.DeviceIdType.MESH,
        )

    def weight_copies(c):
        cols = pl.ds(pl.multiple_of(c * ch, ch), ch)
        return (
            pltpu.make_async_copy(gate_w.at[:, cols], weights.at[c, :, pl.ds(0, ch)], ws.at[c, 0]),
            pltpu.make_async_copy(up_w.at[:, cols], weights.at[c, :, pl.ds(ch, ch)], ws.at[c, 1]),
        )

    def cot_copy(c):
        return pltpu.make_async_copy(cot.at[:, pl.ds(pl.multiple_of(c * ch, ch), ch)], cot_v.at[c], cs.at[c])

    def hid_copy(c):
        return pltpu.make_async_copy(hid_v.at[c], hidden_out.at[:, pl.ds(pl.multiple_of(c * ch, ch), ch)], hs.at[c])

    own_copy = pltpu.make_async_copy(inputs, toks.at[col], zs.at[8])
    own_copy.start()

    @pl.loop(0, chunks)
    def _(c):
        for copy in weight_copies(c):
            copy.start()

    @pl.loop(0, chunks)
    def _(c):
        cot_copy(c).start()

    barrier = pltpu.get_barrier_semaphore()
    for dev in (left_x, right_x, left_y, right_y, left_z, right_z, sibling):
        pl.semaphore_signal(barrier, inc=1, device_id=dev, device_id_type=pl.DeviceIdType.MESH)
    pl.semaphore_wait(barrier, 7)

    mine, from_m, from_p, from_2 = z * 2 + core, zm * 2 + core, zp * 2 + core, z2 * 2 + core
    lo, hi = pl.ds(0, 32), pl.ds(32, 32)

    def spread(src, dst, k, dev):
        return remote(src, dst, zs.at[k], zr.at[k], dev)

    g_left = spread(inputs, toks.at[mine], 0, left_z)
    g_right = spread(inputs, toks.at[mine], 1, right_z)
    g_sib = spread(inputs, toks.at[mine], 2, sibling)
    g_left.start()
    g_right.start()
    g_sib.start()

    def mask(c):
        for copy in weight_copies(c):
            copy.wait()
        for which, pat in enumerate((gate_pat, up_pat)):
            for i in range(weights.shape[1] // BLOCK):
                for j in range(ch // BLOCK):
                    flag = pat[i, c * (ch // BLOCK) + j].astype(F32)
                    rows, cols = pl.ds(i * BLOCK, BLOCK), pl.ds(which * ch + j * BLOCK, BLOCK)
                    weights[c, rows, cols] = (weights[c, rows, cols].astype(F32) * flag).astype(BF16)

    acc[...] = jnp.zeros(acc.shape, F32)
    mask(0)
    g_left.wait_recv()
    f_left = spread(toks.at[from_p, hi], toks.at[from_p, hi], 3, left_z)
    f_left.start()
    s_p = spread(toks.at[from_p], toks.at[from_p], 5, sibling)
    s_p.start()
    g_right.wait_recv()
    f_right = spread(toks.at[from_m, lo], toks.at[from_m, lo], 4, right_z)
    f_right.start()
    s_m = spread(toks.at[from_m], toks.at[from_m], 6, sibling)
    s_m.start()
    f_left.wait_recv()
    f_right.wait_recv()
    s_2 = spread(toks.at[from_2], toks.at[from_2], 7, sibling)
    s_2.start()
    own_copy.wait()
    for copy in (g_sib, s_p, s_m, s_2):
        copy.wait_recv()

    def copies(c, k):
        a, b = pl.ds(0, ch), pl.ds(ch, ch)
        al, ar, bl, br = pl.ds(0, hc), pl.ds(hc, hc), pl.ds(ch, hc), pl.ds(ch + hc, hc)
        first, second, every = pl.ds(0, 2), pl.ds(2, 2), pl.ds(0, 4)
        rows = pl.ds(0, 32)
        xdev, ydev = (left_x, right_x), (left_y, right_y)
        if k == 0:
            srcs = (part.at[c, 0, first, x2], part.at[c, 0, second, x2], part.at[c, 1, y2, first], part.at[c, 1, y2, second])
            dsts = tuple(half1.at[c, i // 2, i % 2] for i in range(4))
            devs = xdev + ydev
        elif k == 1:
            srcs = (part.at[c, 0, every, xm], part.at[c, 0, every, xp], part.at[c, 1, ym], part.at[c, 1, yp])
            dsts = tuple(full1.at[c, i // 2, i % 2] for i in range(4))
            devs = xdev + ydev
        elif k == 2:
            srcs = (
                sum1.at[c, 0, y2, rows, al], sum1.at[c, 0, y2, rows, ar],
                sum1.at[c, 1, x2, rows, al], sum1.at[c, 1, x2, rows, ar],
            )
            dsts = tuple(half2.at[c, i // 2, i % 2] for i in range(4))
            devs = ydev + xdev
        elif k == 3:
            srcs = (sum1.at[c, 0, ym], sum1.at[c, 0, yp], sum1.at[c, 1, xm], sum1.at[c, 1, xp])
            dsts = tuple(full2.at[c, i // 2, i % 2] for i in range(4))
            devs = ydev + xdev
        elif k == 4:
            ga, gb = grads.at[c, y, x, rows, a], grads.at[c, y, x, rows, b]
            srcs = dsts = (ga, ga, gb, gb)
            devs = ydev + xdev
        elif k == 5:
            srcs = dsts = (
                grads.at[c, yp, x, rows, ar], grads.at[c, ym, x, rows, al],
                grads.at[c, y, xp, rows, br], grads.at[c, y, xm, rows, bl],
            )
            devs = ydev + xdev
        elif k == 6:
            ga, gb = grads.at[c, every, x, rows, a], grads.at[c, y, every, rows, b]
            srcs = dsts = (ga, ga, gb, gb)
            devs = xdev + ydev
        else:
            srcs = dsts = (
                grads.at[c, second, xp, rows, a], grads.at[c, first, xm, rows, a],
                grads.at[c, yp, second, rows, b], grads.at[c, ym, first, rows, b],
            )
            devs = xdev + ydev
        return [
            remote(s, d, send.at[c, 4 * k + i], recv.at[c, 4 * k + i], dev)
            for i, (s, d, dev) in enumerate(zip(srcs, dsts, devs))
        ]

    def start(c, k):
        for copy in copies(c, k):
            copy.start()

    def arrived(c, k):
        for copy in copies(c, k):
            copy.wait_recv()

    def f(v):
        return v.astype(F32)

    def forward(c):
        product = jnp.dot(
            toks[...].reshape(8 * 64, toks.shape[2]), weights[c], preferred_element_type=F32
        ).astype(BF16).reshape(4, 4, 32, 2 * ch)
        part[c, 0] = product[:, :, :, :ch]
        part[c, 1] = product[:, :, :, ch:]
        start(c, 0)

    def merge1(c):
        arrived(c, 0)
        part[c, 0, 0:2, xm] = (f(part[c, 0, 0:2, xm]) + f(half1[c, 0, 0])).astype(BF16)
        part[c, 0, 2:4, xp] = (f(part[c, 0, 2:4, xp]) + f(half1[c, 0, 1])).astype(BF16)
        part[c, 1, ym, 0:2] = (f(part[c, 1, ym, 0:2]) + f(half1[c, 1, 0])).astype(BF16)
        part[c, 1, yp, 2:4] = (f(part[c, 1, yp, 2:4]) + f(half1[c, 1, 1])).astype(BF16)
        start(c, 1)

    def total1(c):
        arrived(c, 1)
        sum1[c, 0] = (f(part[c, 0, :, x]) + f(full1[c, 0, 0]) + f(full1[c, 0, 1])).astype(BF16)
        sum1[c, 1] = (f(part[c, 1, y]) + f(full1[c, 1, 0]) + f(full1[c, 1, 1])).astype(BF16)
        start(c, 2)

    def merge2(c):
        arrived(c, 2)
        for i, (m, p) in enumerate(((ym, yp), (xm, xp))):
            sum1[c, i, m, :, 0:hc] = (f(sum1[c, i, m, :, 0:hc]) + f(half2[c, i, 0])).astype(BF16)
            sum1[c, i, p, :, hc:ch] = (f(sum1[c, i, p, :, hc:ch]) + f(half2[c, i, 1])).astype(BF16)
        start(c, 3)

    def activate(c):
        arrived(c, 3)
        cot_copy(c).wait()
        gate_sum = f(sum1[c, 0, y]) + f(full2[c, 0, 0]) + f(full2[c, 0, 1])
        up_sum = f(sum1[c, 1, x]) + f(full2[c, 1, 0]) + f(full2[c, 1, 1])
        sigmoid_gate = jax.nn.sigmoid(gate_sum)
        activated = gate_sum * sigmoid_gate
        cot_f = f(cot_v[c])
        grads[c, y, x, :, 0:ch] = (
            cot_f * up_sum * sigmoid_gate * (1.0 + gate_sum * (1.0 - sigmoid_gate))
        ).astype(BF16)
        grads[c, y, x, :, ch:2 * ch] = (cot_f * activated).astype(BF16)
        start(c, 4)
        hid_v[c] = (activated * up_sum).astype(BF16)
        hid_copy(c).start()

    def forward1(c):
        arrived(c, 4)
        start(c, 5)

    def spread2(c):
        arrived(c, 5)
        start(c, 6)

    def forward2(c):
        arrived(c, 6)
        start(c, 7)

    width = toks.shape[2] // PIECES

    def back(c, n):
        return lax.dot_general(
            grads[c].reshape(512, 2 * ch), weights[c, pl.ds(n * width, width), :],
            (((1,), (1,)), ((), ())), preferred_element_type=F32,
        ).reshape(4, 2, 64, width)

    def backward(c):
        arrived(c, 7)
        for n in range(PIECES):
            acc[n] += back(c, n)

    def masked_forward(c):
        @pl.when(c > 0)
        def _():
            mask(c)

        forward(c)

    stages = (masked_forward, merge1, total1, merge2, activate, forward1, spread2, forward2, backward)
    order = (0, 2, 3, 4, 5, 6, 7, 1, 8)
    steps = chunks + LAGS[8]

    @pl.loop(0, steps - 1)
    def _(step):
        for k in order:
            c = step - LAGS[k]
            last = chunks - 1 if k == 8 else chunks

            @pl.when((c >= 0) & (c < last))
            def _():
                stages[k](c)

    for k in range(1, 8):
        for c in range(max(0, steps - 1 - LAGS[k]), chunks):
            stages[k](c)

    final = chunks - 1
    arrived(final, 7)

    def z_sib(n):
        return remote(zsend.at[n], zsib.at[n], zs.at[9 + n], zr.at[9 + n], sibling)

    base1, base2 = 9 + PIECES, 9 + 3 * PIECES

    def z_half(n):
        return (
            remote(zsend.at[n, z2, lo], zhalf.at[n, 0], zs.at[base1 + 2 * n], zr.at[base1 + 2 * n], left_z),
            remote(zsend.at[n, z2, hi], zhalf.at[n, 1], zs.at[base1 + 2 * n + 1], zr.at[base1 + 2 * n + 1], right_z),
        )

    def z_full(n):
        return (
            remote(zsend.at[n, zm], zfull.at[n, 0], zs.at[base2 + 2 * n], zr.at[base2 + 2 * n], left_z),
            remote(zsend.at[n, zp], zfull.at[n, 1], zs.at[base2 + 2 * n + 1], zr.at[base2 + 2 * n + 1], right_z),
        )

    def out_copy(n):
        return pltpu.make_async_copy(out_v.at[n], grad_out.at[:, pl.ds(n * width, width)], os.at[n])

    def piece_a(n):
        acc[n] += back(final, n)
        zsend[n] = acc[n, :, other].astype(BF16)
        z_sib(n).start()

    def piece_b(n):
        z_sib(n).wait()
        acc[n, :, core] += f(zsib[n])
        zsend[n] = acc[n, :, core].astype(BF16)
        for copy in z_half(n):
            copy.start()

    def piece_c(n):
        for copy in z_half(n):
            copy.wait_recv()
        zsend[n, zm, 0:32] = (acc[n, zm, core, 0:32] + f(zhalf[n, 0])).astype(BF16)
        zsend[n, zp, 32:64] = (acc[n, zp, core, 32:64] + f(zhalf[n, 1])).astype(BF16)
        for copy in z_full(n):
            copy.start()

    def piece_d(n):
        for copy in z_full(n):
            copy.wait_recv()
        out_v[n] = (acc[n, z, core] + f(zfull[n, 0]) + f(zfull[n, 1])).astype(BF16)
        out_copy(n).start()

    for step in range(PIECES + 3):
        for lag, piece in enumerate((piece_a, piece_b, piece_c, piece_d)):
            if 0 <= step - lag < PIECES:
                piece(step - lag)

    for copy in (g_left, g_right, g_sib, f_left, f_right, s_p, s_m, s_2):
        copy.wait_send()
    for n in range(PIECES):
        for copy in z_half(n) + z_full(n):
            copy.wait_send()
        out_copy(n).wait()

    @pl.loop(0, chunks)
    def _(c):
        for k in range(8):
            for copy in copies(c, k):
                copy.wait_send()
        hid_copy(c).wait()


def shards(inputs, gate_weight, up_weight, gate_pattern, up_pattern, cotangent):
    tokens, depth = inputs.shape
    hidden = gate_weight.shape[1]
    chunks = hidden // CHUNK
    ch = CHUNK
    width = depth // PIECES
    any_spec = pl.BlockSpec(memory_space=pl.ANY)
    smem = pl.BlockSpec(memory_space=pltpu.SMEM)
    dma = pltpu.SemaphoreType.DMA
    scratch = [
        pltpu.VMEM((8, tokens, depth), BF16),
        pltpu.VMEM((chunks, depth, 2 * ch), BF16),
        pltpu.VMEM((chunks, 2, 4, 4, 32, ch), BF16),
        pltpu.VMEM((chunks, 2, 2, 2, 32, ch), BF16),
        pltpu.VMEM((chunks, 2, 2, 4, 32, ch), BF16),
        pltpu.VMEM((chunks, 2, 4, 32, ch), BF16),
        pltpu.VMEM((chunks, 2, 2, 32, ch // 2), BF16),
        pltpu.VMEM((chunks, 2, 2, 32, ch), BF16),
        pltpu.VMEM((chunks, 4, 4, 32, 2 * ch), BF16),
        pltpu.VMEM((PIECES, 4, 2, 64, width), F32),
        pltpu.VMEM((PIECES, 4, 64, width), BF16),
        pltpu.VMEM((PIECES, 4, 64, width), BF16),
        pltpu.VMEM((PIECES, 2, 32, width), BF16),
        pltpu.VMEM((PIECES, 2, 64, width), BF16),
        pltpu.VMEM((chunks, 32, ch), BF16),
        pltpu.VMEM((chunks, 32, ch), BF16),
        pltpu.VMEM((PIECES, 64, width), BF16),
        dma((chunks, 32)),
        dma((chunks, 32)),
        dma((9 + 5 * PIECES,)),
        dma((9 + 5 * PIECES,)),
        dma((chunks, 2)),
        dma((chunks,)),
        dma((chunks,)),
        dma((PIECES,)),
    ]
    return pl.pallas_call(
        functools.partial(kernel, chunks),
        out_shape=(
            jax.ShapeDtypeStruct((32, hidden), BF16),
            jax.ShapeDtypeStruct((tokens, depth), BF16),
        ),
        in_specs=[any_spec, any_spec, any_spec, smem, smem, any_spec],
        out_specs=(any_spec, any_spec),
        scratch_shapes=scratch,
        compiler_params=pltpu.CompilerParams(
            collective_id=0, has_side_effects=True, vmem_limit_bytes=58 * 1024 * 1024
        ),
        cost_estimate=pl.CostEstimate(
            flops=4 * 512 * depth * 2 * hidden, bytes_accessed=4 * depth * hidden, transcendentals=32 * hidden
        ),
    )(inputs, gate_weight, up_weight, gate_pattern, up_pattern, cotangent)


def solution(mesh):
    placed = (
        P("col", "row"),
        P("row", "col"),
        P("row", "col"),
        P("row", "col"),
        P("row", "col"),
        P("row", "col"),
    )
    return jax.shard_map(
        shards,
        mesh=mesh,
        in_specs=placed,
        out_specs=(P("row", "col"), P("col", "row")),
        check_vma=False,
    )
```

time: 268 us -> 151 us (0.56)
  waiting for transfers between devices: 180 us -> 0 us
  Pallas kernels: 0 us -> 147 us
  local copies, waits for them, and re-layouts: 34.4 us -> 3.2 us
  matrix products: 28.3 us -> 0 us
  between operations: 13.8 us -> 0.64 us
  other arithmetic: 9.88 us -> 0 us
    pallas_call x0 -> x1, Pallas kernels: none -> 147 us  [shards(): pl.pallas_call(functools.partial(kernel, chunks), out_shape=(jax.ShapeDty...]
    reduce_scatter x2 -> x0, waiting for transfers between devices: 117 us -> none  [the longest x1 84.7 us: shards(): lax.psum_scatter(partial_sums.astype(jnp.bfloat16), 'row', scatter_dimens...]
    all_gather x2 -> x0, waiting for transfers between devices: 63 us -> none  [the longest x1 63 us: shards(): lax.all_gather(gradients, 'row', axis=0, tiled=True)]
    unnamed x11 -> x2, local copies, waits for them, and re-layouts: 32.3 us -> 3.2 us
    dot_general x2 -> x0, matrix products: 28.3 us -> none  [the longest x1 15.2 us: shards(): jnp.dot(lax.all_gather(inputs, 'col', axis=0, tiled=True), stacked_weight...]
    mul x1 -> x0, other arithmetic: 5.73 us -> none  [expand(): weight.reshape(height // BLOCK, BLOCK, breadth // BLOCK, BLOCK)]
    convert_element_type x4 -> x0, other arithmetic: 3.37 us -> none  [the longest x2 1.38 us: expand(): flags = pattern.astype(weight.dtype)]
  transfers between devices with their start and end apart: 4 -> 0, of which waited for: 3 -> 0; matrix products, arithmetic and copies ran while one was open for 11% -> 0% of each run, Pallas kernels for 0% -> 0%
where the time goes in v1:
time: 151 us
  Pallas kernels  147 us (97%)
  local copies, waits for them, and re-layouts  3.2 us (2%)
    pallas_call x1, Pallas kernels, shards(): pl.pallas_call(functools.partial(kernel, chunks), out_shape=(jax.ShapeDty...  147 us
    unnamed x2, local copies, waits for them, and re-layouts  3.2 us

profile of v1, /device:TPU:0, one launch (start us, length us, event | category | flops | bytes accessed | tf_op | source)
XLA Modules:
  0.0 150.6 jit_solution(14579847469879124847)
XLA Ops:
  0.6 146.7 %shard_map.77 = (bf16[32,3328]{1,0:T(8,128)(2,1)}, bf16[64,1024]{1,0:T(8,128)(2,1)}) custom-call(bf16[64,1024]{1,0:T(8,128)(2,1)} %inputs.1, bf16[1024,3328]{1,0:T(8,128)(2,1)} %gate_w.1, bf16[1024,3328]{1,0:T(8,128)(2,1)} %up_w.1, s32[8,26]{1,0:T(8,128)} %gate_pat.1, s32[8,26]{1,0:T(8,128)} %up_pat.1, bf16[32,3328]{1,0:T(8,128)(2,1)} %cot.1), custom_call_target="tpu_custom_call" | custom-call | flops 13958643712 | bytes 13631488 | tf_op jit(solution)/shard_map/pallas_call | solution.py:383
  147.4 1.6 %copy.10 = bf16[32,3328]{1,0:T(8,128)(2,1)} copy(bf16[32,3328]{1,0:T(8,128)(2,1)} %get-tuple-element.4) | data formatting | bytes 425984
  149.0 1.6 %copy.11 = bf16[64,1024]{1,0:T(8,128)(2,1)} copy(bf16[64,1024]{1,0:T(8,128)(2,1)} %get-tuple-element.5) | data formatting | bytes 262144

commit v2 on v1

--- a/solution.py
+++ b/solution.py
@@ -11,15 +11,15 @@
 SIDE = 4
 CHUNK = 256
 PIECES = 4
-LAGS = (0, 1, 2, 3, 4, 5, 6, 7, 8)
+LAGS = (0, 4, 8, 12, 16, 20, 24, 28, 32)
 F32 = jnp.float32
 BF16 = jnp.bfloat16
 
 
 def kernel(
     chunks, inputs, gate_w, up_w, gate_pat, up_pat, cot, hidden_out, grad_out,
-    toks, weights, part, half1, full1, sum1, half2, full2, grads, acc, zsend, zsib, zhalf, zfull,
-    cot_v, hid_v, out_v, send, recv, zs, zr, ws, cs, hs, os,
+    toks, weights, part, half1, full1, sum1, half2, full2, grads, acc, zsend, zsib, zkeep, zhalf, zfull,
+    cot_v, hid_v, out_v, send, recv, zsent, zin, zout, ws, local,
 ):
     ch = CHUNK
     hc = ch // 2
@@ -49,17 +49,17 @@
     def weight_copies(c):
         cols = pl.ds(pl.multiple_of(c * ch, ch), ch)
         return (
-            pltpu.make_async_copy(gate_w.at[:, cols], weights.at[c, :, pl.ds(0, ch)], ws.at[c, 0]),
-            pltpu.make_async_copy(up_w.at[:, cols], weights.at[c, :, pl.ds(ch, ch)], ws.at[c, 1]),
+            pltpu.make_async_copy(gate_w.at[:, cols], weights.at[c, :, pl.ds(0, ch)], ws.at[c]),
+            pltpu.make_async_copy(up_w.at[:, cols], weights.at[c, :, pl.ds(ch, ch)], ws.at[c]),
         )
 
     def cot_copy(c):
-        return pltpu.make_async_copy(cot.at[:, pl.ds(pl.multiple_of(c * ch, ch), ch)], cot_v.at[c], cs.at[c])
+        return pltpu.make_async_copy(cot.at[:, pl.ds(pl.multiple_of(c * ch, ch), ch)], cot_v.at[c], local.at[1])
 
     def hid_copy(c):
-        return pltpu.make_async_copy(hid_v.at[c], hidden_out.at[:, pl.ds(pl.multiple_of(c * ch, ch), ch)], hs.at[c])
-
-    own_copy = pltpu.make_async_copy(inputs, toks.at[col], zs.at[8])
+        return pltpu.make_async_copy(hid_v.at[c], hidden_out.at[:, pl.ds(pl.multiple_of(c * ch, ch), ch)], local.at[2])
+
+    own_copy = pltpu.make_async_copy(inputs, toks.at[col], local.at[0])
     own_copy.start()
 
     @pl.loop(0, chunks)
@@ -74,24 +74,14 @@
     barrier = pltpu.get_barrier_semaphore()
     for dev in (left_x, right_x, left_y, right_y, left_z, right_z, sibling):
         pl.semaphore_signal(barrier, inc=1, device_id=dev, device_id_type=pl.DeviceIdType.MESH)
-    pl.semaphore_wait(barrier, 7)
-
-    mine, from_m, from_p, from_2 = z * 2 + core, zm * 2 + core, zp * 2 + core, z2 * 2 + core
-    lo, hi = pl.ds(0, 32), pl.ds(32, 32)
-
-    def spread(src, dst, k, dev):
-        return remote(src, dst, zs.at[k], zr.at[k], dev)
-
-    g_left = spread(inputs, toks.at[mine], 0, left_z)
-    g_right = spread(inputs, toks.at[mine], 1, right_z)
-    g_sib = spread(inputs, toks.at[mine], 2, sibling)
-    g_left.start()
-    g_right.start()
-    g_sib.start()
+    def all_landed(ref, sem):
+        remote(ref, ref, sem, sem, sibling).wait_recv()
+
+    def all_left(ref, sem):
+        remote(ref, ref, sem, sem, sibling).wait_send()
 
     def mask(c):
-        for copy in weight_copies(c):
-            copy.wait()
+        pltpu.make_async_copy(weights.at[c], weights.at[c], ws.at[c]).wait()
         for which, pat in enumerate((gate_pat, up_pat)):
             for i in range(weights.shape[1] // BLOCK):
                 for j in range(ch // BLOCK):
@@ -99,24 +89,51 @@
                     rows, cols = pl.ds(i * BLOCK, BLOCK), pl.ds(which * ch + j * BLOCK, BLOCK)
                     weights[c, rows, cols] = (weights[c, rows, cols].astype(F32) * flag).astype(BF16)
 
+    def mask_some(part_of):
+        pl.loop(part_of * chunks // 3, (part_of + 1) * chunks // 3)(mask)
+
+    mask_some(0)
+    pl.semaphore_wait(barrier, 7)
+
+    mine, from_m, from_p, from_2 = z * 2 + core, zm * 2 + core, zp * 2 + core, z2 * 2 + core
+    lo, hi = pl.ds(0, 32), pl.ds(32, 32)
+
+    def spread(src, dst, k, dev):
+        return remote(src, dst, zsent.at[0], zin.at[k], dev)
+
+    def from_input(rows, k, dev):
+        return spread(inputs.at[rows], toks.at[mine, rows], k, dev)
+
+    def onward(block, rows, k, dev):
+        return spread(toks.at[block, rows], toks.at[block, rows], k, dev)
+
+    whole = pl.ds(0, 64)
+    to_left_hi, to_right_lo = from_input(hi, 0, left_z), from_input(lo, 2, right_z)
+    to_left_lo, to_right_hi = from_input(lo, 1, left_z), from_input(hi, 3, right_z)
+    to_sibling = from_input(whole, 4, sibling)
+    for copy in (to_left_hi, to_right_lo, to_left_lo, to_right_hi, to_sibling):
+        copy.start()
     acc[...] = jnp.zeros(acc.shape, F32)
-    mask(0)
-    g_left.wait_recv()
-    f_left = spread(toks.at[from_p, hi], toks.at[from_p, hi], 3, left_z)
-    f_left.start()
-    s_p = spread(toks.at[from_p], toks.at[from_p], 5, sibling)
-    s_p.start()
-    g_right.wait_recv()
-    f_right = spread(toks.at[from_m, lo], toks.at[from_m, lo], 4, right_z)
-    f_right.start()
-    s_m = spread(toks.at[from_m], toks.at[from_m], 6, sibling)
-    s_m.start()
-    f_left.wait_recv()
-    f_right.wait_recv()
-    s_2 = spread(toks.at[from_2], toks.at[from_2], 7, sibling)
-    s_2.start()
+    mask_some(1)
+    on_left, on_right = onward(from_p, hi, 5, left_z), onward(from_m, lo, 6, right_z)
+    to_left_hi.wait_recv()
+    on_left.start()
+    to_right_lo.wait_recv()
+    on_right.start()
+    share_p, share_m = onward(from_p, whole, 7, sibling), onward(from_m, whole, 8, sibling)
+    share_2hi, share_2lo = onward(from_2, hi, 9, sibling), onward(from_2, lo, 10, sibling)
+    to_left_lo.wait_recv()
+    share_p.start()
+    to_right_hi.wait_recv()
+    share_m.start()
+    mask_some(2)
+    on_left.wait_recv()
+    share_2hi.start()
+    on_right.wait_recv()
+    share_2lo.start()
     own_copy.wait()
-    for copy in (g_sib, s_p, s_m, s_2):
+    pltpu.make_async_copy(cot_v, cot_v, local.at[1]).wait()
+    for copy in (to_sibling, share_p, share_m, share_2hi, share_2lo):
         copy.wait_recv()
 
     def copies(c, k):
@@ -165,17 +182,18 @@
             )
             devs = xdev + ydev
         return [
-            remote(s, d, send.at[c, 4 * k + i], recv.at[c, 4 * k + i], dev)
-            for i, (s, d, dev) in enumerate(zip(srcs, dsts, devs))
+            remote(s, d, send.at[k], recv.at[c, k], dev)
+            for s, d, dev in zip(srcs, dsts, devs)
         ]
 
     def start(c, k):
         for copy in copies(c, k):
             copy.start()
 
+    sizes = (half1, full1, half2, full2, full2, half2, full1, half1)
+
     def arrived(c, k):
-        for copy in copies(c, k):
-            copy.wait_recv()
+        all_landed(sizes[k].at[c], recv.at[c, k])
 
     def f(v):
         return v.astype(F32)
@@ -211,7 +229,6 @@
 
     def activate(c):
         arrived(c, 3)
-        cot_copy(c).wait()
         gate_sum = f(sum1[c, 0, y]) + f(full2[c, 0, 0]) + f(full2[c, 0, 1])
         up_sum = f(sum1[c, 1, x]) + f(full2[c, 1, 0]) + f(full2[c, 1, 1])
         sigmoid_gate = jax.nn.sigmoid(gate_sum)
@@ -250,15 +267,8 @@
         for n in range(PIECES):
             acc[n] += back(c, n)
 
-    def masked_forward(c):
-        @pl.when(c > 0)
-        def _():
-            mask(c)
-
-        forward(c)
-
-    stages = (masked_forward, merge1, total1, merge2, activate, forward1, spread2, forward2, backward)
-    order = (0, 2, 3, 4, 5, 6, 7, 1, 8)
+    stages = (forward, merge1, total1, merge2, activate, forward1, spread2, forward2, backward)
+    order = (7, 6, 5, 4, 3, 2, 1, 0, 8)
     steps = chunks + LAGS[8]
 
     @pl.loop(0, steps - 1)
@@ -278,25 +288,26 @@
     final = chunks - 1
     arrived(final, 7)
 
+    def z_send(src, dst, k, n, dev):
+        return remote(src, dst, zsent.at[1], zout.at[k, n], dev)
+
     def z_sib(n):
-        return remote(zsend.at[n], zsib.at[n], zs.at[9 + n], zr.at[9 + n], sibling)
-
-    base1, base2 = 9 + PIECES, 9 + 3 * PIECES
+        return z_send(zsend.at[n], zsib.at[n], 0, n, sibling)
 
     def z_half(n):
         return (
-            remote(zsend.at[n, z2, lo], zhalf.at[n, 0], zs.at[base1 + 2 * n], zr.at[base1 + 2 * n], left_z),
-            remote(zsend.at[n, z2, hi], zhalf.at[n, 1], zs.at[base1 + 2 * n + 1], zr.at[base1 + 2 * n + 1], right_z),
+            z_send(zkeep.at[n, z2, lo], zhalf.at[n, 0], 1, n, left_z),
+            z_send(zkeep.at[n, z2, hi], zhalf.at[n, 1], 1, n, right_z),
         )
 
     def z_full(n):
         return (
-            remote(zsend.at[n, zm], zfull.at[n, 0], zs.at[base2 + 2 * n], zr.at[base2 + 2 * n], left_z),
-            remote(zsend.at[n, zp], zfull.at[n, 1], zs.at[base2 + 2 * n + 1], zr.at[base2 + 2 * n + 1], right_z),
+            z_send(zkeep.at[n, zm], zfull.at[n, 0], 2, n, left_z),
+            z_send(zkeep.at[n, zp], zfull.at[n, 1], 2, n, right_z),
         )
 
     def out_copy(n):
-        return pltpu.make_async_copy(out_v.at[n], grad_out.at[:, pl.ds(n * width, width)], os.at[n])
+        return pltpu.make_async_copy(out_v.at[n], grad_out.at[:, pl.ds(n * width, width)], local.at[3])
 
     def piece_a(n):
         acc[n] += back(final, n)
@@ -304,23 +315,22 @@
         z_sib(n).start()
 
     def piece_b(n):
-        z_sib(n).wait()
-        acc[n, :, core] += f(zsib[n])
-        zsend[n] = acc[n, :, core].astype(BF16)
+        all_landed(zsib.at[n], zout.at[0, n])
+        total = acc[n, :, core] + f(zsib[n])
+        acc[n, :, core] = total
+        zkeep[n] = total.astype(BF16)
         for copy in z_half(n):
             copy.start()
 
     def piece_c(n):
-        for copy in z_half(n):
-            copy.wait_recv()
-        zsend[n, zm, 0:32] = (acc[n, zm, core, 0:32] + f(zhalf[n, 0])).astype(BF16)
-        zsend[n, zp, 32:64] = (acc[n, zp, core, 32:64] + f(zhalf[n, 1])).astype(BF16)
+        all_landed(zhalf.at[n], zout.at[1, n])
+        zkeep[n, zm, 0:32] = (acc[n, zm, core, 0:32] + f(zhalf[n, 0])).astype(BF16)
+        zkeep[n, zp, 32:64] = (acc[n, zp, core, 32:64] + f(zhalf[n, 1])).astype(BF16)
         for copy in z_full(n):
             copy.start()
 
     def piece_d(n):
-        for copy in z_full(n):
-            copy.wait_recv()
+        all_landed(zfull.at[n], zout.at[2, n])
         out_v[n] = (acc[n, z, core] + f(zfull[n, 0]) + f(zfull[n, 1])).astype(BF16)
         out_copy(n).start()
 
@@ -329,19 +339,12 @@
             if 0 <= step - lag < PIECES:
                 piece(step - lag)
 
-    for copy in (g_left, g_right, g_sib, f_left, f_right, s_p, s_m, s_2):
-        copy.wait_send()
-    for n in range(PIECES):
-        for copy in z_half(n) + z_full(n):
-            copy.wait_send()
-        out_copy(n).wait()
-
-    @pl.loop(0, chunks)
-    def _(c):
-        for k in range(8):
-            for copy in copies(c, k):
-                copy.wait_send()
-        hid_copy(c).wait()
+    for k in range(8):
+        all_left(sizes[k], send.at[k])
+    for k in range(2):
+        all_left(toks.at[pl.ds(0, 7)], zsent.at[k])
+    pltpu.make_async_copy(hid_v, hid_v, local.at[2]).wait()
+    pltpu.make_async_copy(out_v, out_v, local.at[3]).wait()
 
 
 def shards(inputs, gate_weight, up_weight, gate_pattern, up_pattern, cotangent):
@@ -366,19 +369,19 @@
         pltpu.VMEM((PIECES, 4, 2, 64, width), F32),
         pltpu.VMEM((PIECES, 4, 64, width), BF16),
         pltpu.VMEM((PIECES, 4, 64, width), BF16),
+        pltpu.VMEM((PIECES, 4, 64, width), BF16),
         pltpu.VMEM((PIECES, 2, 32, width), BF16),
         pltpu.VMEM((PIECES, 2, 64, width), BF16),
         pltpu.VMEM((chunks, 32, ch), BF16),
         pltpu.VMEM((chunks, 32, ch), BF16),
         pltpu.VMEM((PIECES, 64, width), BF16),
-        dma((chunks, 32)),
-        dma((chunks, 32)),
-        dma((9 + 5 * PIECES,)),
-        dma((9 + 5 * PIECES,)),
-        dma((chunks, 2)),
+        dma((8,)),
+        dma((chunks, 8)),
+        dma((2,)),
+        dma((11,)),
+        dma((3, PIECES)),
         dma((chunks,)),
-        dma((chunks,)),
-        dma((PIECES,)),
+        dma((4,)),
     ]
     return pl.pallas_call(
         functools.partial(kernel, chunks),

time: 151 us -> 112 us (0.74)
  Pallas kernels: 147 us -> 108 us
    pallas_call x1, Pallas kernels: 147 us -> 108 us  [shards(): pl.pallas_call(functools.partial(kernel, chunks), out_shape=(jax.ShapeDty...]
where the time goes in v2:
time: 112 us
  Pallas kernels  108 us (96%)
  local copies, waits for them, and re-layouts  3.2 us (3%)
    pallas_call x1, Pallas kernels, shards(): pl.pallas_call(functools.partial(kernel, chunks), out_shape=(jax.ShapeDty...  108 us
    unnamed x2, local copies, waits for them, and re-layouts  3.2 us

profile of v2, /device:TPU:0, one launch (start us, length us, event | category | flops | bytes accessed | tf_op | source)
XLA Modules:
  0.0 111.6 jit_solution(9943806544111641758)
XLA Ops:
  0.6 107.7 %shard_map.77 = (bf16[32,3328]{1,0:T(8,128)(2,1)}, bf16[64,1024]{1,0:T(8,128)(2,1)}) custom-call(bf16[64,1024]{1,0:T(8,128)(2,1)} %inputs.1, bf16[1024,3328]{1,0:T(8,128)(2,1)} %gate_w.1, bf16[1024,3328]{1,0:T(8,128)(2,1)} %up_w.1, s32[8,26]{1,0:T(8,128)} %gate_pat.1, s32[8,26]{1,0:T(8,128)} %up_pat.1, bf16[32,3328]{1,0:T(8,128)(2,1)} %cot.1), custom_call_target="tpu_custom_call" | custom-call | flops 13958643712 | bytes 13631488 | tf_op jit(solution)/shard_map/pallas_call | solution.py:386
  108.4 1.6 %copy.10 = bf16[32,3328]{1,0:T(8,128)(2,1)} copy(bf16[32,3328]{1,0:T(8,128)(2,1)} %get-tuple-element.4) | data formatting | bytes 425984
  110.0 1.6 %copy.11 = bf16[64,1024]{1,0:T(8,128)(2,1)} copy(bf16[64,1024]{1,0:T(8,128)(2,1)} %get-tuple-element.5) | data formatting | bytes 262144

commit v3 on v2

--- a/solution.py
+++ b/solution.py
@@ -334,10 +334,9 @@
         out_v[n] = (acc[n, z, core] + f(zfull[n, 0]) + f(zfull[n, 1])).astype(BF16)
         out_copy(n).start()
 
-    for step in range(PIECES + 3):
-        for lag, piece in enumerate((piece_a, piece_b, piece_c, piece_d)):
-            if 0 <= step - lag < PIECES:
-                piece(step - lag)
+    for piece in (piece_a, piece_b, piece_c, piece_d):
+        for n in range(PIECES):
+            piece(n)
 
     for k in range(8):
         all_left(sizes[k], send.at[k])
@@ -345,6 +344,11 @@
         all_left(toks.at[pl.ds(0, 7)], zsent.at[k])
     pltpu.make_async_copy(hid_v, hid_v, local.at[2]).wait()
     pltpu.make_async_copy(out_v, out_v, local.at[3]).wait()
+
+
+def hand_over(hidden, grad, hidden_out, grad_out):
+    hidden_out[...] = hidden[...]
+    grad_out[...] = grad[...]
 
 
 def shards(inputs, gate_weight, up_weight, gate_pattern, up_pattern, cotangent):
@@ -383,7 +387,7 @@
         dma((chunks,)),
         dma((4,)),
     ]
-    return pl.pallas_call(
+    results = pl.pallas_call(
         functools.partial(kernel, chunks),
         out_shape=(
             jax.ShapeDtypeStruct((32, hidden), BF16),
@@ -399,6 +403,12 @@
             flops=4 * 512 * depth * 2 * hidden, bytes_accessed=4 * depth * hidden, transcendentals=32 * hidden
         ),
     )(inputs, gate_weight, up_weight, gate_pattern, up_pattern, cotangent)
+    return pl.pallas_call(
+        hand_over,
+        out_shape=tuple(jax.ShapeDtypeStruct(r.shape, r.dtype) for r in results),
+        in_specs=[pl.BlockSpec(memory_space=pltpu.VMEM)] * 2,
+        out_specs=(pl.BlockSpec(memory_space=pltpu.VMEM),) * 2,
+    )(*results)
 
 
 def solution(mesh):

time: 112 us -> 105 us (0.938)
  Pallas kernels: 108 us -> 104 us
  local copies, waits for them, and re-layouts: 3.2 us -> 0 us
    pallas_call x1, Pallas kernels: 108 us -> 103 us  [shards(): pl.pallas_call(functools.partial(kernel, chunks), out_shape=(jax.ShapeDty...]
    unnamed x2 -> x0, local copies, waits for them, and re-layouts: 3.2 us -> none
    pallas_call x0 -> x1, Pallas kernels: none -> 1.75 us  [shards(): pl.pallas_call(hand_over, out_shape=tuple((jax.ShapeDtypeStruct(r.shape,...]
where the time goes in v3:
time: 105 us
  Pallas kernels  104 us (99%)
    pallas_call x1, Pallas kernels, shards(): pl.pallas_call(functools.partial(kernel, chunks), out_shape=(jax.ShapeDty...  103 us

profile of v3, /device:TPU:0, one launch (start us, length us, event | category | flops | bytes accessed | tf_op | source)
XLA Modules:
  0.0 105.0 jit_solution(13129362896732004789)
XLA Ops:
  0.6 102.6 %shard_map.77 = (bf16[32,3328]{1,0:T(8,128)(2,1)}, bf16[64,1024]{1,0:T(8,128)(2,1)}) custom-call(bf16[64,1024]{1,0:T(8,128)(2,1)} %inputs.1, bf16[1024,3328]{1,0:T(8,128)(2,1)} %gate_w.1, bf16[1024,3328]{1,0:T(8,128)(2,1)} %up_w.1, s32[8,26]{1,0:T(8,128)} %gate_pat.1, s32[8,26]{1,0:T(8,128)} %up_pat.1, bf16[32,3328]{1,0:T(8,128)(2,1)} %cot.1), custom_call_target="tpu_custom_call" | custom-call | flops 13958643712 | bytes 13631488 | tf_op jit(solution)/shard_map/pallas_call | solution.py:390
  103.2 1.8 %shard_map.78 = (bf16[32,3328]{1,0:T(8,128)(2,1)}, bf16[64,1024]{1,0:T(8,128)(2,1)}) custom-call(bf16[32,3328]{1,0:T(8,128)(2,1)} %get-tuple-element.4.hidden, bf16[64,1024]{1,0:T(8,128)(2,1)} %get-tuple-element.5.grad), custom_call_target="tpu_custom_call" | custom-call | tf_op jit(solution)/shard_map/pallas_call | solution.py:406

commit v4 on v3

--- a/solution.py
+++ b/solution.py
@@ -10,15 +10,18 @@
 BLOCK = 128
 SIDE = 4
 CHUNK = 256
-PIECES = 4
-LAGS = (0, 4, 8, 12, 16, 20, 24, 28, 32)
+GATHER_AT = (5, 9)
+SUM_AFTER = (0, 2, 9)
+HALF = 16
+PIECES = 2
+LAGS = (0, 5, 10, 15, 20, 25, 30, 35, 40)
 F32 = jnp.float32
 BF16 = jnp.bfloat16
 
 
 def kernel(
     chunks, inputs, gate_w, up_w, gate_pat, up_pat, cot, hidden_out, grad_out,
-    toks, weights, part, half1, full1, sum1, half2, full2, grads, acc, zsend, zsib, zkeep, zhalf, zfull,
+    toks, weights, part, half1, full1, sum1, half2, full2, grads, acc, zsend, zsib, zkeep, zfull,
     cot_v, hid_v, out_v, send, recv, zsent, zin, zout, ws, local,
 ):
     ch = CHUNK
@@ -38,7 +41,7 @@
         return (row, zz * 2 + cc)
 
     left_x, right_x, left_y, right_y = at(y, xm), at(y, xp), at(ym, x), at(yp, x)
-    left_z, right_z, sibling = atz(zm, core), atz(zp, core), atz(z, other)
+    left_z, right_z, far_z, sibling = atz(zm, core), atz(zp, core), atz(z2, core), atz(z, other)
 
     def remote(src, dst, s, r, dev):
         return pltpu.make_async_remote_copy(
@@ -53,26 +56,39 @@
             pltpu.make_async_copy(up_w.at[:, cols], weights.at[c, :, pl.ds(ch, ch)], ws.at[c]),
         )
 
+    units = 2 * chunks
+
+    def half_of(u):
+        return lax.div(u, chunks)
+
+    def chunk_of(u):
+        return lax.rem(u, chunks)
+
+    def strip(ref, u):
+        rows = pl.ds(pl.multiple_of(half_of(u) * HALF, HALF), HALF)
+        return ref.at[rows, pl.ds(pl.multiple_of(chunk_of(u) * ch, ch), ch)]
+
     def cot_copy(c):
-        return pltpu.make_async_copy(cot.at[:, pl.ds(pl.multiple_of(c * ch, ch), ch)], cot_v.at[c], local.at[1])
+        return pltpu.make_async_copy(strip(cot, c), cot_v.at[c], local.at[1])
 
     def hid_copy(c):
-        return pltpu.make_async_copy(hid_v.at[c], hidden_out.at[:, pl.ds(pl.multiple_of(c * ch, ch), ch)], local.at[2])
-
-    own_copy = pltpu.make_async_copy(inputs, toks.at[col], local.at[0])
-    own_copy.start()
+        return pltpu.make_async_copy(hid_v.at[c], strip(hidden_out, c), local.at[2])
+
+    own_copies = [pltpu.make_async_copy(inputs.at[:, h], toks.at[h, col], local.at[0]) for h in range(2)]
+    for copy in own_copies:
+        copy.start()
 
     @pl.loop(0, chunks)
     def _(c):
         for copy in weight_copies(c):
             copy.start()
 
-    @pl.loop(0, chunks)
-    def _(c):
-        cot_copy(c).start()
+    @pl.loop(0, units)
+    def _(u):
+        cot_copy(u).start()
 
     barrier = pltpu.get_barrier_semaphore()
-    for dev in (left_x, right_x, left_y, right_y, left_z, right_z, sibling):
+    for dev in (left_x, right_x, left_y, right_y, left_z, right_z, far_z, sibling):
         pl.semaphore_signal(barrier, inc=1, device_id=dev, device_id_type=pl.DeviceIdType.MESH)
     def all_landed(ref, sem):
         remote(ref, ref, sem, sem, sibling).wait_recv()
@@ -93,54 +109,51 @@
         pl.loop(part_of * chunks // 3, (part_of + 1) * chunks // 3)(mask)
 
     mask_some(0)
-    pl.semaphore_wait(barrier, 7)
+    pl.semaphore_wait(barrier, 8)
 
     mine, from_m, from_p, from_2 = z * 2 + core, zm * 2 + core, zp * 2 + core, z2 * 2 + core
-    lo, hi = pl.ds(0, 32), pl.ds(32, 32)
-
-    def spread(src, dst, k, dev):
-        return remote(src, dst, zsent.at[0], zin.at[k], dev)
-
-    def from_input(rows, k, dev):
-        return spread(inputs.at[rows], toks.at[mine, rows], k, dev)
-
-    def onward(block, rows, k, dev):
-        return spread(toks.at[block, rows], toks.at[block, rows], k, dev)
-
-    whole = pl.ds(0, 64)
-    to_left_hi, to_right_lo = from_input(hi, 0, left_z), from_input(lo, 2, right_z)
-    to_left_lo, to_right_hi = from_input(lo, 1, left_z), from_input(hi, 3, right_z)
-    to_sibling = from_input(whole, 4, sibling)
-    for copy in (to_left_hi, to_right_lo, to_left_lo, to_right_hi, to_sibling):
-        copy.start()
+    both = pl.ds(0, 2)
+
+    def spread(h, src, block, k, dev):
+        dst = toks.at[h, block]
+        return remote(dst if src is None else src, dst, zsent.at[0], zin.at[h, k], dev)
+
+    def own_sends(h):
+        devs = (far_z, left_z, right_z, sibling)
+        return [spread(h, inputs.at[:, h], mine, k, dev) for k, dev in enumerate(devs)]
+
+    def shares(h):
+        return [spread(h, None, block, 4 + k, sibling) for k, block in enumerate((from_2, from_p, from_m))]
+
+    def gather_start(h):
+        for copy in own_sends(h):
+            copy.start()
+
+    def gather_share(h):
+        for k in (1, 2, 0):
+            own_sends(h)[k].wait_recv()
+            shares(h)[k].start()
+
+    def gather_end(h):
+        own_sends(h)[3].wait_recv()
+        for copy in shares(h):
+            copy.wait_recv()
+
+    gather_start(0)
     acc[...] = jnp.zeros(acc.shape, F32)
     mask_some(1)
-    on_left, on_right = onward(from_p, hi, 5, left_z), onward(from_m, lo, 6, right_z)
-    to_left_hi.wait_recv()
-    on_left.start()
-    to_right_lo.wait_recv()
-    on_right.start()
-    share_p, share_m = onward(from_p, whole, 7, sibling), onward(from_m, whole, 8, sibling)
-    share_2hi, share_2lo = onward(from_2, hi, 9, sibling), onward(from_2, lo, 10, sibling)
-    to_left_lo.wait_recv()
-    share_p.start()
-    to_right_hi.wait_recv()
-    share_m.start()
+    gather_start(1)
     mask_some(2)
-    on_left.wait_recv()
-    share_2hi.start()
-    on_right.wait_recv()
-    share_2lo.start()
-    own_copy.wait()
+    gather_share(0)
+    pltpu.make_async_copy(toks.at[both, 0], toks.at[both, 0], local.at[0]).wait()
     pltpu.make_async_copy(cot_v, cot_v, local.at[1]).wait()
-    for copy in (to_sibling, share_p, share_m, share_2hi, share_2lo):
-        copy.wait_recv()
+    gather_end(0)
 
     def copies(c, k):
         a, b = pl.ds(0, ch), pl.ds(ch, ch)
         al, ar, bl, br = pl.ds(0, hc), pl.ds(hc, hc), pl.ds(ch, hc), pl.ds(ch + hc, hc)
         first, second, every = pl.ds(0, 2), pl.ds(2, 2), pl.ds(0, 4)
-        rows = pl.ds(0, 32)
+        rows = pl.ds(0, HALF)
         xdev, ydev = (left_x, right_x), (left_y, right_y)
         if k == 0:
             srcs = (part.at[c, 0, first, x2], part.at[c, 0, second, x2], part.at[c, 1, y2, first], part.at[c, 1, y2, second])
@@ -200,8 +213,8 @@
 
     def forward(c):
         product = jnp.dot(
-            toks[...].reshape(8 * 64, toks.shape[2]), weights[c], preferred_element_type=F32
-        ).astype(BF16).reshape(4, 4, 32, 2 * ch)
+            toks[half_of(c)].reshape(16 * HALF, toks.shape[4]), weights[chunk_of(c)], preferred_element_type=F32
+        ).astype(BF16).reshape(4, 4, HALF, 2 * ch)
         part[c, 0] = product[:, :, :, :ch]
         part[c, 1] = product[:, :, :, ch:]
         start(c, 0)
@@ -254,94 +267,90 @@
         arrived(c, 6)
         start(c, 7)
 
-    width = toks.shape[2] // PIECES
-
-    def back(c, n):
+    width = toks.shape[4] // PIECES
+
+    def back(u, n):
         return lax.dot_general(
-            grads[c].reshape(512, 2 * ch), weights[c, pl.ds(n * width, width), :],
+            grads[u].reshape(16 * HALF, 2 * ch), weights[chunk_of(u), pl.ds(n * width, width), :],
             (((1,), (1,)), ((), ())), preferred_element_type=F32,
-        ).reshape(4, 2, 64, width)
-
-    def backward(c):
-        arrived(c, 7)
+        ).reshape(4, 2, 2, HALF, width)
+
+    def backward(u):
+        arrived(u, 7)
         for n in range(PIECES):
-            acc[n] += back(c, n)
+            acc[n, half_of(u)] += back(u, n)
 
     stages = (forward, merge1, total1, merge2, activate, forward1, spread2, forward2, backward)
-    order = (7, 6, 5, 4, 3, 2, 1, 0, 8)
-    steps = chunks + LAGS[8]
+    final = units - 1
+
+    def z_send(src, dst, k, h, n, dev):
+        return remote(src, dst, zsent.at[1], zout.at[k, h, n], dev)
+
+    def z_sib(h, n):
+        return z_send(zsend.at[h, n], zsib.at[h, n], 0, h, n, sibling)
+
+    def z_full(h, n):
+        pairs = ((z2, far_z), (zm, left_z), (zp, right_z))
+        return [z_send(zkeep.at[h, n, to], zfull.at[h, n, k], 1, h, n, dev) for k, (to, dev) in enumerate(pairs)]
+
+    def out_copy(h, n):
+        return pltpu.make_async_copy(out_v.at[h, n], grad_out.at[:, h, :, pl.ds(n * width, width)], local.at[3])
+
+    def sum_sibling(h, n):
+        zsend[h, n] = acc[n, h, :, other].astype(BF16)
+        z_sib(h, n).start()
+
+    def sum_last(h, n):
+        acc[n, h] += back(final, n)
+        sum_sibling(h, n)
+
+    def sum_cores(h, n):
+        all_landed(zsib.at[h, n], zout.at[0, h, n])
+        total = acc[n, h, :, core] + f(zsib[h, n])
+        acc[n, h, :, core] = total
+        zkeep[h, n] = total.astype(BF16)
+        for copy in z_full(h, n):
+            copy.start()
+
+    def sum_end(h, n):
+        all_landed(zfull.at[h, n], zout.at[1, h, n])
+        terms = acc[n, h, z, core] + f(zfull[h, n, 0]) + f(zfull[h, n, 1]) + f(zfull[h, n, 2])
+        out_v[h, n] = terms.astype(BF16)
+        out_copy(h, n).start()
+
+    order = (0, 1, 2, 3, 4, 5, 6, 7, 8)
+    steps = units + LAGS[8]
+
+    first_done = chunks + LAGS[8]
+    events = [(when, lambda g=g: g(1)) for when, g in zip(GATHER_AT, (gather_share, gather_end))]
+    for after, piece in zip(SUM_AFTER, (sum_sibling, sum_cores, sum_end)):
+        events.append((first_done + after, lambda p=piece: [p(0, n) for n in range(PIECES)]))
 
     @pl.loop(0, steps - 1)
     def _(step):
+        for when, event in events:
+
+            @pl.when(step == when)
+            def _():
+                event()
+
         for k in order:
-            c = step - LAGS[k]
-            last = chunks - 1 if k == 8 else chunks
-
-            @pl.when((c >= 0) & (c < last))
+            u = step - LAGS[k]
+            last = final if k == 8 else units
+
+            @pl.when((u >= 0) & (u < last))
             def _():
-                stages[k](c)
-
-    for k in range(1, 8):
-        for c in range(max(0, steps - 1 - LAGS[k]), chunks):
-            stages[k](c)
-
-    final = chunks - 1
+                stages[k](u)
+
     arrived(final, 7)
-
-    def z_send(src, dst, k, n, dev):
-        return remote(src, dst, zsent.at[1], zout.at[k, n], dev)
-
-    def z_sib(n):
-        return z_send(zsend.at[n], zsib.at[n], 0, n, sibling)
-
-    def z_half(n):
-        return (
-            z_send(zkeep.at[n, z2, lo], zhalf.at[n, 0], 1, n, left_z),
-            z_send(zkeep.at[n, z2, hi], zhalf.at[n, 1], 1, n, right_z),
-        )
-
-    def z_full(n):
-        return (
-            z_send(zkeep.at[n, zm], zfull.at[n, 0], 2, n, left_z),
-            z_send(zkeep.at[n, zp], zfull.at[n, 1], 2, n, right_z),
-        )
-
-    def out_copy(n):
-        return pltpu.make_async_copy(out_v.at[n], grad_out.at[:, pl.ds(n * width, width)], local.at[3])
-
-    def piece_a(n):
-        acc[n] += back(final, n)
-        zsend[n] = acc[n, :, other].astype(BF16)
-        z_sib(n).start()
-
-    def piece_b(n):
-        all_landed(zsib.at[n], zout.at[0, n])
-        total = acc[n, :, core] + f(zsib[n])
-        acc[n, :, core] = total
-        zkeep[n] = total.astype(BF16)
-        for copy in z_half(n):
-            copy.start()
-
-    def piece_c(n):
-        all_landed(zhalf.at[n], zout.at[1, n])
-        zkeep[n, zm, 0:32] = (acc[n, zm, core, 0:32] + f(zhalf[n, 0])).astype(BF16)
-        zkeep[n, zp, 32:64] = (acc[n, zp, core, 32:64] + f(zhalf[n, 1])).astype(BF16)
-        for copy in z_full(n):
-            copy.start()
-
-    def piece_d(n):
-        all_landed(zfull.at[n], zout.at[2, n])
-        out_v[n] = (acc[n, z, core] + f(zfull[n, 0]) + f(zfull[n, 1])).astype(BF16)
-        out_copy(n).start()
-
-    for piece in (piece_a, piece_b, piece_c, piece_d):
+    for piece in (sum_last, sum_cores, sum_end):
         for n in range(PIECES):
-            piece(n)
+            piece(1, n)
 
     for k in range(8):
         all_left(sizes[k], send.at[k])
     for k in range(2):
-        all_left(toks.at[pl.ds(0, 7)], zsent.at[k])
+        all_left(toks.at[both, pl.ds(0, 7)], zsent.at[k])
     pltpu.make_async_copy(hid_v, hid_v, local.at[2]).wait()
     pltpu.make_async_copy(out_v, out_v, local.at[3]).wait()
 
@@ -355,35 +364,35 @@
     tokens, depth = inputs.shape
     hidden = gate_weight.shape[1]
     chunks = hidden // CHUNK
+    units = 2 * chunks
     ch = CHUNK
     width = depth // PIECES
     any_spec = pl.BlockSpec(memory_space=pl.ANY)
     smem = pl.BlockSpec(memory_space=pltpu.SMEM)
     dma = pltpu.SemaphoreType.DMA
     scratch = [
-        pltpu.VMEM((8, tokens, depth), BF16),
+        pltpu.VMEM((2, 8, 2, HALF, depth), BF16),
         pltpu.VMEM((chunks, depth, 2 * ch), BF16),
-        pltpu.VMEM((chunks, 2, 4, 4, 32, ch), BF16),
-        pltpu.VMEM((chunks, 2, 2, 2, 32, ch), BF16),
-        pltpu.VMEM((chunks, 2, 2, 4, 32, ch), BF16),
-        pltpu.VMEM((chunks, 2, 4, 32, ch), BF16),
-        pltpu.VMEM((chunks, 2, 2, 32, ch // 2), BF16),
-        pltpu.VMEM((chunks, 2, 2, 32, ch), BF16),
-        pltpu.VMEM((chunks, 4, 4, 32, 2 * ch), BF16),
-        pltpu.VMEM((PIECES, 4, 2, 64, width), F32),
-        pltpu.VMEM((PIECES, 4, 64, width), BF16),
-        pltpu.VMEM((PIECES, 4, 64, width), BF16),
-        pltpu.VMEM((PIECES, 4, 64, width), BF16),
-        pltpu.VMEM((PIECES, 2, 32, width), BF16),
-        pltpu.VMEM((PIECES, 2, 64, width), BF16),
-        pltpu.VMEM((chunks, 32, ch), BF16),
-        pltpu.VMEM((chunks, 32, ch), BF16),
-        pltpu.VMEM((PIECES, 64, width), BF16),
+        pltpu.VMEM((units, 2, 4, 4, HALF, ch), BF16),
+        pltpu.VMEM((units, 2, 2, 2, HALF, ch), BF16),
+        pltpu.VMEM((units, 2, 2, 4, HALF, ch), BF16),
+        pltpu.VMEM((units, 2, 4, HALF, ch), BF16),
+        pltpu.VMEM((units, 2, 2, HALF, ch // 2), BF16),
+        pltpu.VMEM((units, 2, 2, HALF, ch), BF16),
+        pltpu.VMEM((units, 4, 4, HALF, 2 * ch), BF16),
+        pltpu.VMEM((PIECES, 2, 4, 2, 2, HALF, width), F32),
+        pltpu.VMEM((2, PIECES, 4, 2, HALF, width), BF16),
+        pltpu.VMEM((2, PIECES, 4, 2, HALF, width), BF16),
+        pltpu.VMEM((2, PIECES, 4, 2, HALF, width), BF16),
+        pltpu.VMEM((2, PIECES, 3, 2, HALF, width), BF16),
+        pltpu.VMEM((units, HALF, ch), BF16),
+        pltpu.VMEM((units, HALF, ch), BF16),
+        pltpu.VMEM((2, PIECES, 2, HALF, width), BF16),
         dma((8,)),
-        dma((chunks, 8)),
+        dma((units, 8)),
         dma((2,)),
-        dma((11,)),
-        dma((3, PIECES)),
+        dma((2, 7)),
+        dma((2, 2, PIECES)),
         dma((chunks,)),
         dma((4,)),
     ]
@@ -391,7 +400,7 @@
         functools.partial(kernel, chunks),
         out_shape=(
             jax.ShapeDtypeStruct((32, hidden), BF16),
-            jax.ShapeDtypeStruct((tokens, depth), BF16),
+            jax.ShapeDtypeStruct((2, 2, HALF, depth), BF16),
         ),
         in_specs=[any_spec, any_spec, any_spec, smem, smem, any_spec],
         out_specs=(any_spec, any_spec),
@@ -402,7 +411,8 @@
         cost_estimate=pl.CostEstimate(
             flops=4 * 512 * depth * 2 * hidden, bytes_accessed=4 * depth * hidden, transcendentals=32 * hidden
         ),
-    )(inputs, gate_weight, up_weight, gate_pattern, up_pattern, cotangent)
+    )(inputs.reshape(2, 2, HALF, depth), gate_weight, up_weight, gate_pattern, up_pattern, cotangent)
+    results = (results[0], results[1].reshape(tokens, depth))
     return pl.pallas_call(
         hand_over,
         out_shape=tuple(jax.ShapeDtypeStruct(r.shape, r.dtype) for r in results),

time: 105 us -> 102 us (0.971)
  Pallas kernels: 104 us -> 101 us
    pallas_call x1, Pallas kernels: 103 us -> 98.9 us  [shards(): pl.pallas_call(functools.partial(kernel, chunks), out_shape=(jax.ShapeDty...]
where the time goes in v4:
time: 102 us; the launch traced here: 101 us
  Pallas kernels  101 us (99%)
    pallas_call x1, Pallas kernels, shards(): pl.pallas_call(functools.partial(kernel, chunks), out_shape=(jax.ShapeDty...  98.9 us

profile of v4, /device:TPU:0, one launch (start us, length us, event | category | flops | bytes accessed | tf_op | source)
XLA Modules:
  0.0 101.3 jit_solution(1034697321165767881)
XLA Ops:
  0.6 98.9 %shard_map.77 = (bf16[32,3328]{1,0:T(8,128)(2,1)}, bf16[2,2,16,1024]{3,2,1,0:T(8,128)(2,1)}) custom-call(bf16[2,2,16,1024]{3,2,1,0:T(8,128)(2,1)} %bitcast.3, bf16[1024,3328]{1,0:T(8,128)(2,1)} %gate_w.1, bf16[1024,3328]{1,0:T(8,128)(2,1)} %up_w.1, s32[8,26]{1,0:T(8,128)} %gate_pat.1, s32[8,26]{1,0:T(8,128)} %up_pat.1, bf16[32,3328]{1,0:T(8,128)(2,1)} %cot.1), custom_call_target="tpu_custom_call" | custom-call | flops 13958643712 | bytes 13631488 | tf_op jit(solution)/shard_map/pallas_call | solution.py:399
  99.5 1.8 %shard_map.78 = (bf16[32,3328]{1,0:T(8,128)(2,1)}, bf16[64,1024]{1,0:T(8,128)(2,1)}) custom-call(bf16[32,3328]{1,0:T(8,128)(2,1)} %get-tuple-element.4.hidden, bf16[64,1024]{1,0:T(8,128)(2,1)} %bitcast.2), custom_call_target="tpu_custom_call" | custom-call | tf_op jit(solution)/shard_map/pallas_call | solution.py:416

commit v5 on v4

--- a/solution.py
+++ b/solution.py
@@ -195,7 +195,7 @@
             )
             devs = xdev + ydev
         return [
-            remote(s, d, send.at[k], recv.at[c, k], dev)
+            remote(s, d, send.at[k], recv.at[chunk_of(c), k], dev)
             for s, d, dev in zip(srcs, dsts, devs)
         ]
 
@@ -206,7 +206,7 @@
     sizes = (half1, full1, half2, full2, full2, half2, full1, half1)
 
     def arrived(c, k):
-        all_landed(sizes[k].at[c], recv.at[c, k])
+        all_landed(sizes[k].at[c], recv.at[chunk_of(c), k])
 
     def f(v):
         return v.astype(F32)
@@ -389,7 +389,7 @@
         pltpu.VMEM((units, HALF, ch), BF16),
         pltpu.VMEM((2, PIECES, 2, HALF, width), BF16),
         dma((8,)),
-        dma((units, 8)),
+        dma((chunks, 8)),
         dma((2,)),
         dma((2, 7)),
         dma((2, 2, PIECES)),

time: 102 us -> 101 us (level)
  Pallas kernels: 101 us -> 99.8 us
where the time goes in v5:
time: 101 us; the launch traced here: 100 us
  Pallas kernels  99.8 us (99%)
    pallas_call x1, Pallas kernels, shards(): pl.pallas_call(functools.partial(kernel, chunks), out_shape=(jax.ShapeDty...  98 us

profile of v5, /device:TPU:0, one launch (start us, length us, event | category | flops | bytes accessed | tf_op | source)
XLA Modules:
  0.0 100.4 jit_solution(6780755034914396211)
XLA Ops:
  0.6 98.0 %shard_map.77 = (bf16[32,3328]{1,0:T(8,128)(2,1)}, bf16[2,2,16,1024]{3,2,1,0:T(8,128)(2,1)}) custom-call(bf16[2,2,16,1024]{3,2,1,0:T(8,128)(2,1)} %bitcast.3, bf16[1024,3328]{1,0:T(8,128)(2,1)} %gate_w.1, bf16[1024,3328]{1,0:T(8,128)(2,1)} %up_w.1, s32[8,26]{1,0:T(8,128)} %gate_pat.1, s32[8,26]{1,0:T(8,128)} %up_pat.1, bf16[32,3328]{1,0:T(8,128)(2,1)} %cot.1), custom_call_target="tpu_custom_call" | custom-call | flops 13958643712 | bytes 13631488 | tf_op jit(solution)/shard_map/pallas_call | solution.py:399
  98.7 1.8 %shard_map.78 = (bf16[32,3328]{1,0:T(8,128)(2,1)}, bf16[64,1024]{1,0:T(8,128)(2,1)}) custom-call(bf16[32,3328]{1,0:T(8,128)(2,1)} %get-tuple-element.4.hidden, bf16[64,1024]{1,0:T(8,128)(2,1)} %bitcast.2), custom_call_target="tpu_custom_call" | custom-call | tf_op jit(solution)/shard_map/pallas_call | solution.py:416

commit v6 on v5

--- a/solution.py
+++ b/solution.py
@@ -143,7 +143,6 @@
     acc[...] = jnp.zeros(acc.shape, F32)
     mask_some(1)
     gather_start(1)
-    mask_some(2)
     gather_share(0)
     pltpu.make_async_copy(toks.at[both, 0], toks.at[both, 0], local.at[0]).wait()
     pltpu.make_async_copy(cot_v, cot_v, local.at[1]).wait()
@@ -328,6 +327,10 @@
 
     @pl.loop(0, steps - 1)
     def _(step):
+        @pl.when((step >= 2 * chunks // 3) & (step < chunks))
+        def _():
+            mask(step)
+
         for when, event in events:
 
             @pl.when(step == when)

time: 101 us -> 101 us (level)
  no operation moved by 1% of the time
where the time goes in v6:
time: 101 us; the launch traced here: 100 us
  Pallas kernels  99.8 us (99%)
    pallas_call x1, Pallas kernels, shards(): pl.pallas_call(functools.partial(kernel, chunks), out_shape=(jax.ShapeDty...  98.1 us

profile of v6, /device:TPU:0, one launch (start us, length us, event | category | flops | bytes accessed | tf_op | source)
XLA Modules:
  0.0 100.5 jit_solution(3140480719734019679)
XLA Ops:
  0.6 98.1 %shard_map.77 = (bf16[32,3328]{1,0:T(8,128)(2,1)}, bf16[2,2,16,1024]{3,2,1,0:T(8,128)(2,1)}) custom-call(bf16[2,2,16,1024]{3,2,1,0:T(8,128)(2,1)} %bitcast.3, bf16[1024,3328]{1,0:T(8,128)(2,1)} %gate_w.1, bf16[1024,3328]{1,0:T(8,128)(2,1)} %up_w.1, s32[8,26]{1,0:T(8,128)} %gate_pat.1, s32[8,26]{1,0:T(8,128)} %up_pat.1, bf16[32,3328]{1,0:T(8,128)(2,1)} %cot.1), custom_call_target="tpu_custom_call" | custom-call | flops 13958643712 | bytes 13631488 | tf_op jit(solution)/shard_map/pallas_call | solution.py:402
  98.7 1.8 %shard_map.78 = (bf16[32,3328]{1,0:T(8,128)(2,1)}, bf16[64,1024]{1,0:T(8,128)(2,1)}) custom-call(bf16[32,3328]{1,0:T(8,128)(2,1)} %get-tuple-element.4.hidden, bf16[64,1024]{1,0:T(8,128)(2,1)} %bitcast.2), custom_call_target="tpu_custom_call" | custom-call | tf_op jit(solution)/shard_map/pallas_call | solution.py:419

commit v7 on v6

--- a/solution.py
+++ b/solution.py
@@ -126,8 +126,9 @@
         return [spread(h, None, block, 4 + k, sibling) for k, block in enumerate((from_2, from_p, from_m))]
 
     def gather_start(h):
-        for copy in own_sends(h):
-            copy.start()
+        sends = own_sends(h)
+        for k in (1, 2, 0, 3):
+            sends[k].start()
 
     def gather_share(h):
         for k in (1, 2, 0):

time: 101 us -> 102 us (level)
  no operation moved by 1% of the time
where the time goes in v7:
time: 102 us; the launch traced here: 101 us
  Pallas kernels  100 us (98%)
    pallas_call x1, Pallas kernels, shards(): pl.pallas_call(functools.partial(kernel, chunks), out_shape=(jax.ShapeDty...  98.4 us

profile of v7, /device:TPU:0, one launch (start us, length us, event | category | flops | bytes accessed | tf_op | source)
XLA Modules:
  0.0 100.8 jit_solution(2888174438350731442)
XLA Ops:
  0.6 98.4 %shard_map.77 = (bf16[32,3328]{1,0:T(8,128)(2,1)}, bf16[2,2,16,1024]{3,2,1,0:T(8,128)(2,1)}) custom-call(bf16[2,2,16,1024]{3,2,1,0:T(8,128)(2,1)} %bitcast.3, bf16[1024,3328]{1,0:T(8,128)(2,1)} %gate_w.1, bf16[1024,3328]{1,0:T(8,128)(2,1)} %up_w.1, s32[8,26]{1,0:T(8,128)} %gate_pat.1, s32[8,26]{1,0:T(8,128)} %up_pat.1, bf16[32,3328]{1,0:T(8,128)(2,1)} %cot.1), custom_call_target="tpu_custom_call" | custom-call | flops 13958643712 | bytes 13631488 | tf_op jit(solution)/shard_map/pallas_call | solution.py:403
  99.1 1.8 %shard_map.78 = (bf16[32,3328]{1,0:T(8,128)(2,1)}, bf16[64,1024]{1,0:T(8,128)(2,1)}) custom-call(bf16[32,3328]{1,0:T(8,128)(2,1)} %get-tuple-element.4.hidden, bf16[64,1024]{1,0:T(8,128)(2,1)} %bitcast.2), custom_call_target="tpu_custom_call" | custom-call | tf_op jit(solution)/shard_map/pallas_call | solution.py:420
